TPU v7x, 256 devices: a whole 4x4x8 slice. The times are simulated.
256 devices in a mesh: kv: 32 (over x, y, core), dp: 8 (over z).
Axes of the slice: x: 4, y: 4, z: 8, core: 2. Of those that a mesh axis runs over, the one named last changes fastest.
Arguments:
- queries: bfloat16 [64, 128, 576], P('dp'), may hold values from -48 to 48
- drafts: bfloat16 [64, 576], P('dp'), may hold values from -18 to 18
- cache: bfloat16 [16, 131072, 576], P('dp', 'kv'), may hold values from -4 to 4
- lengths: int32 [16], P('dp'), may hold values from 65536 to 131072, as said below
- row_seq: int32 [64], P('dp'), may hold values from 0 to 1, as said below
- row_pos: int32 [64], P('dp'), may hold values from 65536 to 131075, as said below
- w_uv: bfloat16 [128, 512, 128], P('kv'), may hold values from -0.25 to 0.25
- w_out: bfloat16 [16384, 7168], P('kv', 'dp'), may hold values from -0.046875 to 0.046875
- hidden: bfloat16 [64, 7168], P(None, 'dp'), may hold values from -0.59765625 to 0.59765625
- gain: float32 [7168], P('dp'), may hold values from 0.1 to 1.9
- w_gate: bfloat16 [7168, 18432], P('dp', 'kv'), may hold values from -0.0625 to 0.0625
- w_up: bfloat16 [7168, 18432], P('dp', 'kv'), may hold values from -0.0625 to 0.0625
- w_down: bfloat16 [18432, 7168], P('kv', 'dp'), may hold values from -0.01171875 to 0.01171875
Outputs:
- mixed: bfloat16 [64, 7168], P(None, 'dp')
Inputs may be any that keep to these rules, and one draw needn't show every extreme that they name: `lengths`: sequence 0 has exactly 131072 live positions. `row_seq`: each of a group's 2 sequences owns exactly 4 rows of the group, in any order. `row_pos`: A row's position is its sequence's length plus a step number; the 4 rows of one sequence take the step numbers 0 to 3 once each.
All inputs are finite; a program needn't handle non-finite values.
Results may differ from a plain program's by a relative error of at most 0.009.
Values may be sent and summed in bfloat16 or wider, within the bound.
A program may use at most 128 MiB of HBM per device.

v0:
```python
import jax
import jax.numpy as jnp
from jax import lax
from jax.sharding import PartitionSpec as P

D = 7168
LAT = 512
ROPE = 64
HD = 128
SEQ_DP = 2
STEPS = 4


def scan_cache(query_rows, key_rows, live_len, block_len, block_count):
    qk_scale = (HD + ROPE) ** (-0.5)
    row_count = query_rows.shape[0]

    def visit(block_idx, carry):
        run_max, run_sum, weighted = carry
        key_block = lax.dynamic_slice_in_dim(key_rows, block_idx * block_len, block_len, 0)
        scores = (
            jnp.einsum("rc,kc->rk", query_rows, key_block, preferred_element_type=jnp.float32)
            * qk_scale
        )
        valid = block_idx * block_len + jnp.arange(block_len) < live_len
        scores = jnp.where(valid[None, :], scores, -1e30)
        new_max = jnp.maximum(run_max, jnp.max(scores, axis=1))
        weights = jnp.where(valid[None, :], jnp.exp(scores - new_max[:, None]), 0.0)
        factor = jnp.exp(run_max - new_max)
        run_sum = run_sum * factor + jnp.sum(weights, axis=1)
        weighted = weighted * factor[:, None] + jnp.dot(
            weights.astype(jnp.bfloat16), key_block[:, :LAT], preferred_element_type=jnp.float32
        )
        return (new_max, run_sum, weighted)

    start_carry = (
        jnp.full((row_count,), -1e30, jnp.float32),
        jnp.zeros((row_count,), jnp.float32),
        jnp.zeros((row_count, LAT), jnp.float32),
    )
    return lax.fori_loop(0, block_count, visit, start_carry)


def on_device(
    queries,
    drafts,
    cache,
    lengths,
    row_seq,
    row_pos,
    w_uv,
    w_out,
    hidden,
    gain,
    w_gate,
    w_up,
    w_down,
):
    kv_count = lax.axis_size("kv")
    kv_index = lax.axis_index("kv")
    tok_group, head_count = (queries.shape[0], queries.shape[1])
    head_local = head_count // kv_count
    ctx_dev = cache.shape[1]
    shard_start = kv_index * ctx_dev
    block_len = min(512, ctx_dev)
    block_total = ctx_dev // block_len
    qk_scale = (HD + ROPE) ** (-0.5)
    order_idx = jnp.arange(tok_group)
    same_seq = row_seq[:, None] == row_seq[None, :]
    rank_in_seq = jnp.sum(same_seq & (order_idx[:, None] > order_idx[None, :]), axis=1)
    picker = (row_seq[None, None, :] == jnp.arange(SEQ_DP)[:, None, None]) & (
        rank_in_seq[None, None, :] == jnp.arange(STEPS)[None, :, None]
    )
    picker_b = picker.astype(jnp.bfloat16)
    sorted_q = jnp.einsum(
        "sri,ihc->srhc", picker_b, queries, preferred_element_type=jnp.float32
    ).astype(jnp.bfloat16)
    sorted_drafts = (
        jnp.einsum("sri,ic->src", picker_b, drafts, preferred_element_type=jnp.float32)
        .astype(jnp.bfloat16)
        .reshape(tok_group, -1)
    )
    sorted_pos = jnp.sum(jnp.where(picker, row_pos[None, None, :], 0), axis=2).reshape(-1)
    sorted_seq = jnp.repeat(jnp.arange(SEQ_DP), STEPS)
    max_parts, sum_parts, acc_parts = ([], [], [])
    for seq_idx in range(SEQ_DP):
        live_len = lengths[seq_idx] - shard_start
        query_rows = sorted_q[seq_idx].reshape(STEPS * head_count, -1)
        run_max, run_sum, weighted = scan_cache(
            query_rows, cache[seq_idx], live_len, block_len, block_total
        )
        max_parts.append(run_max.reshape(STEPS, head_count))
        sum_parts.append(run_sum.reshape(STEPS, head_count))
        acc_parts.append(weighted.reshape(STEPS, head_count, LAT))
    local_max = jnp.concatenate(max_parts, axis=0)
    local_sum = jnp.concatenate(sum_parts, axis=0)
    local_acc = jnp.concatenate(acc_parts, axis=0)
    recv_acc, recv_max, recv_sum = (
        lax.all_to_all(local_acc[None], "kv", split_axis=2, concat_axis=0, tiled=True),
        lax.all_to_all(local_max[None], "kv", split_axis=2, concat_axis=0, tiled=True),
        lax.all_to_all(local_sum[None], "kv", split_axis=2, concat_axis=0, tiled=True),
    )
    head_max = jnp.max(recv_max, axis=0)
    rescale = jnp.exp(recv_max - head_max[None])
    head_acc = jnp.sum(recv_acc * rescale[..., None], axis=0)
    head_sum = jnp.sum(recv_sum * rescale, axis=0)
    head_q = lax.dynamic_slice_in_dim(
        sorted_q.reshape(tok_group, head_count, -1), kv_index * head_local, head_local, 1
    )
    draft_scores = (
        jnp.einsum("thc,jc->thj", head_q, sorted_drafts, preferred_element_type=jnp.float32)
        * qk_scale
    )
    draft_valid = (sorted_seq[:, None] == sorted_seq[None, :]) & (
        sorted_pos[None, :] <= sorted_pos[:, None]
    )
    draft_scores = jnp.where(draft_valid[:, None, :], draft_scores, -1e30)
    final_max = jnp.maximum(head_max, jnp.max(draft_scores, axis=2))
    adjust = jnp.exp(head_max - final_max)
    draft_weight = jnp.where(
        draft_valid[:, None, :], jnp.exp(draft_scores - final_max[:, :, None]), 0.0
    )
    denom = head_sum * adjust + jnp.sum(draft_weight, axis=2)
    numer = head_acc * adjust[:, :, None] + jnp.einsum(
        "thj,jl->thl",
        draft_weight.astype(jnp.bfloat16),
        sorted_drafts[:, :LAT],
        preferred_element_type=jnp.float32,
    )
    latent_sorted = (
        (numer / denom[:, :, None]).astype(jnp.bfloat16).reshape(SEQ_DP, STEPS, head_local, LAT)
    )
    latent_rows = jnp.einsum(
        "sri,srhl->ihl", picker_b, latent_sorted, preferred_element_type=jnp.float32
    ).astype(jnp.bfloat16)
    all_latents = lax.all_gather(latent_rows, "dp", axis=0, tiled=True)
    all_values = jnp.einsum(
        "thl,hlv->thv", all_latents, w_uv, preferred_element_type=jnp.float32
    ).astype(jnp.bfloat16)
    row_total = all_values.shape[0]
    attn_part = jnp.dot(
        all_values.reshape(row_total, head_local * HD), w_out, preferred_element_type=jnp.float32
    )
    attended = lax.psum(attn_part, "kv")
    resid = (hidden.astype(jnp.float32) + attended).astype(jnp.bfloat16)
    resid_f = resid.astype(jnp.float32)
    square_part = jnp.sum(resid_f * resid_f, axis=1)
    scaled = (resid_f * gain[None, :]).astype(jnp.bfloat16)
    gate_part = jnp.dot(scaled, w_gate, preferred_element_type=jnp.float32)
    up_part = jnp.dot(scaled, w_up, preferred_element_type=jnp.float32)
    gate_sum, up_sum, square_sum = lax.psum((gate_part, up_part, square_part), "dp")
    inv_rms = lax.rsqrt(square_sum / D + 1e-06)[:, None]
    act = (jax.nn.silu(gate_sum * inv_rms) * (up_sum * inv_rms)).astype(jnp.bfloat16)
    down_part = jnp.dot(act, w_down, preferred_element_type=jnp.float32)
    down_sum = lax.psum(down_part, "kv")
    return (resid_f + down_sum).astype(jnp.bfloat16)


def solution(mesh):
    placed = (
        P("dp", None, None),
        P("dp", None),
        P("dp", "kv", None),
        P("dp"),
        P("dp"),
        P("dp"),
        P("kv", None, None),
        P("kv", "dp"),
        P(None, "dp"),
        P("dp"),
        P("dp", "kv"),
        P("dp", "kv"),
        P("kv", "dp"),
    )
    return jax.shard_map(
        on_device, mesh=mesh, in_specs=placed, out_specs=P(None, "dp"), check_vma=False
    )
```

profile of v0, /device:TPU:1, one launch (start us, length us, event | category | flops | bytes accessed | tf_op | source)
XLA Modules:
  0.0 512.8 jit_solution(558890728346907678)
XLA Ops:
  8.1 1.3 fusion.69
  9.5 8.8 %fusion.67 = (bf16[1,4096,576]{1,2,0:T(8,128)(2,1)}, bf16[1,4096,576]{1,2,0:T(8,128)(2,1)}) fusion(bf16[2,4096,576]{1,2,0:T(8,128)(2,1)} %param.19), kind=kLoop, calls=%fused_computation.110 | loop fusion | bytes 18874368 | tf_op jit(solution)/shard_map/slice | solution.py:90
  18.3 7.7 %copy.93 = bf16[1,4096,576]{2,1,0:T(8,128)(2,1)} copy(bf16[1,4096,576]{1,2,0:T(8,128)(2,1)} %get-tuple-element.440) | data formatting | bytes 9437184
  27.0 1.0 copy-done.1
  28.0 1.2 fusion.68
  29.2 1.5 copy.91
  31.2 40.8 %while.37 = (s32[]{:T(128)}, f32[512]{0:T(512)S(1)}, f32[512]{0:T(512)S(1)}, f32[512,512]{1,0:T(8,128)}, s32[]{:T(128)}, /*index=5*/bf16[4096,576]{1,0:T(8,128)(...) while((s32[]{:T(128)}, f32[512]{0:T(512)S(1)}, ...), condition=%wide.region_8.9_spmd.clone, body=%wide.region_5.0_spmd.clone.sunk | while | flops 573574656 | bytes 7112895 | solution.py:41
  31.3 1.9 fusion.103
  33.5 2.6 convolution_add_fusion.6
  36.1 1.9 fusion.103
  38.2 3.0 convolution_add_fusion.6
  41.2 1.9 fusion.103
  43.4 3.0 convolution_add_fusion.6
  46.3 1.9 fusion.103
  48.5 3.0 convolution_add_fusion.6
  51.5 1.9 fusion.103
  53.6 3.0 convolution_add_fusion.6
  56.6 1.9 fusion.103
  58.8 3.0 convolution_add_fusion.6
  61.7 1.9 fusion.103
  63.9 3.0 convolution_add_fusion.6
  66.9 1.9 fusion.103
  69.0 3.0 convolution_add_fusion.6
  72.6 7.7 %copy.92 = bf16[1,4096,576]{2,1,0:T(8,128)(2,1)} copy(bf16[1,4096,576]{1,2,0:T(8,128)(2,1)} %get-tuple-element.439) | data formatting | bytes 9437184
  80.4 1.5 copy.90
  81.8 30.9 %while.36 = (s32[]{:T(128)}, f32[512]{0:T(512)S(1)}, f32[512]{0:T(512)S(1)}, f32[512,512]{1,0:T(8,128)S(1)}, s32[]{:T(128)}, /*index=5*/bf16[4096,576]{1,0:T(8,1...) while((s32[]{:T(128)}, f32[512]{0:T(512)S(1)}, ...), condition=%wide.region_4.5_spmd.clone, body=%wide.region_1.4_spmd.clone.sunk | while | flops 573574656 | bytes 7112895 | solution.py:41
  81.8 1.9 fusion.97
  84.0 1.6 convolution_add_fusion.5
  85.7 1.9 fusion.97
  87.9 1.6 convolution_add_fusion.5
  89.5 1.9 fusion.97
  91.7 1.6 convolution_add_fusion.5
  93.4 1.9 fusion.97
  95.6 1.6 convolution_add_fusion.5
  97.3 1.9 fusion.97
  99.5 1.6 convolution_add_fusion.5
  101.1 1.9 fusion.97
  103.3 1.6 convolution_add_fusion.5
  105.0 1.9 fusion.97
  107.2 1.6 convolution_add_fusion.5
  108.9 1.9 fusion.97
  111.1 1.6 convolution_add_fusion.5
  113.5 8.6 %all-to-all-start.2 = ((f32[1,8,128]{1,0,2:T(1,128)}), f32[1,8,128]{1,0,2:T(1,128)S(1)}, u32[]{:S(2)}, u32[]{:S(2)}) async-start(f32[1,8,128]{1,0,2:T(1,128)} %copy.85), calls=%async_computation.2 | async-start | bytes 131072 | tf_op jit(solution)/shard_map/all_to_all | solution.py:101
  122.8 6.6 %all-to-all-done.2 = f32[1,8,128]{1,0,2:T(1,128)S(1)} async-done(((f32[1,8,128]{1,0,2:T(1,128)}), f32[1,8,128]{1,0,2:T(1,128)S(1)}, u32[]{:S(2)}, u32[]{:S(2)}) %all-to-all-start.2) | async-done | bytes 4128 | tf_op jit(solution)/shard_map/all_to_all | solution.py:101
  129.4 3.9 all-to-all-start.1
  133.3 1.4 maximum_bitcast_fusion
  134.7 2.6 copy.77
  137.3 3.5 all-to-all-done.1
  140.8 4.7 all-to-all-start
  145.8 1.2 copy.81
  147.2 1.7 constant_dynamic-slice_fusion
  150.4 23.6 %all-to-all-done = f32[1,8,128,512]{3,1,0,2:T(8,128)} async-done(((f32[1,8,128,512]{3,1,0,2:T(8,128)}), f32[1,8,128,512]{3,1,0,2:T(8,128)}, u32[]{:S(2)}, u32[]{:S(2)}) %all-to-all-start) | async-done | bytes 2097184 | tf_op jit(solution)/shard_map/all_to_all | solution.py:99
  174.0 3.1 fusion.26
  177.5 22.4 %all_gather.3 = bf16[64,4,512]{2,0,1:T(8,128)(2,1)S(1)} all-gather(bf16[8,4,512]{2,0,1:T(8,128)(2,1)S(1)} %fusion.32), channel_id=1, replica_groups=mesh['kv'=32,'dp'=8] {'dp'}, dimensions={0}, use_global_device_ids=true | all-gather | bytes 294912 | tf_op jit(solution)/shard_map/all_gather | solution.py:136
  200.1 2.2 fusion.44
  202.4 112.3 %all-reduce.5.cloned.1.call-done = f32[64,896]{1,0:T(8,128)} async-done(((f32[64,896]{1,0:T(8,128)}), f32[64,896]{1,0:T(8,128)}) %all-reduce.5.cloned.1.call-update) | async-done | bytes 229392 | tf_op jit(solution)/shard_map/psum | solution.py:144
  314.7 1.1 fusion.35
  315.8 1.1 fusion.37
  316.9 2.3 fusion.39
  319.3 13.8 %psum.37 = f32[64]{0:T(128)S(1)} all-reduce(f32[64]{0:T(128)S(1)} %get-tuple-element.429), channel_id=1, replica_groups=mesh['kv'=32,'dp'=8] {'dp'}, use_global_device_ids=true, to_apply=%region_18.19 | all-reduce | flops 64 | bytes 512 | tf_op jit(solution)/shard_map/psum | solution.py:151
  333.1 54.6 %all-reduce.9.cloned.1.call-done = (f32[64,576]{1,0:T(8,128)}, f32[64,576]{1,0:T(8,128)}) async-done(((f32[64,576]{1,0:T(8,128)}, f32[64,576]{1,0:T(8,128)}), (f32[64,576]{1,0:T(8,128)}, f32[64,576]{1,0:T(8,128)})) %all-reduce.9.cloned.1.call-update) | async-done | bytes 294928 | tf_op jit(solution)/shard_map/psum | solution.py:151
  387.8 2.0 fusion.41
  389.8 114.9 %all-reduce.7.cloned.1.call-done = f32[64,896]{1,0:T(8,128)} async-done(((f32[64,896]{1,0:T(8,128)}), f32[64,896]{1,0:T(8,128)}) %all-reduce.7.cloned.1.call-update) | async-done | bytes 229392 | tf_op jit(solution)/shard_map/psum | solution.py:155
  504.7 1.6 fusion.36
  (142 shorter events, 10.6 us)
Async XLA Ops:
  6.5 381.2 %copy-start = (bf16[576,896]{1,0:T(8,128)(2,1)S(1)}, bf16[576,896]{1,0:T(8,128)(2,1)}, u32[]{:S(2)}) copy-start(bf16[576,896]{1,0:T(8,128)(2,1)} %param.29) | copy-start | bytes 3096580
  18.3 7.8 %copy-start.4 = (bf16[8,128,576]{1,2,0:T(8,128)(2,1)S(1)}, bf16[8,128,576]{1,2,0:T(8,128)(2,1)}, u32[]{:S(2)}) copy-start(bf16[8,128,576]{1,2,0:T(8,128)(2,1)} %param.17) | copy-start | bytes 3538948
  27.0 1.0 copy-start.1
  72.6 7.7 %copy-start.3 = (bf16[1,4,128,576]{2,1,3,0:T(4,128)(2,1)S(1)}, bf16[1,4,128,576]{2,1,3,0:T(4,128)(2,1)}, u32[]{:S(2)}) copy-start(bf16[1,4,128,576]{2,1,3,0:T(4,128)(2,1)} %get-tuple-element.441) | copy-start | bytes 1769476
  113.5 16.0 %all-to-all-start.2 = ((f32[1,8,128]{1,0,2:T(1,128)}), f32[1,8,128]{1,0,2:T(1,128)S(1)}, u32[]{:S(2)}, u32[]{:S(2)}) async-start(f32[1,8,128]{1,0,2:T(1,128)} %copy.85), calls=%async_computation.2 | async-start | bytes 131072 | tf_op jit(solution)/shard_map/all_to_all | solution.py:101
  129.4 11.4 %all-to-all-start.1 = ((f32[1,8,128]{1,0,2:T(1,128)}), f32[1,8,128]{1,0,2:T(1,128)S(1)}, u32[]{:S(2)}, u32[]{:S(2)}) async-start(f32[1,8,128]{1,0,2:T(1,128)} %copy.79), calls=%async_computation.1 | async-start | bytes 131072 | tf_op jit(solution)/shard_map/all_to_all | solution.py:100
  137.3 8.5 %copy-start.2 = (bf16[2,4,128,576]{2,1,3,0:T(4,128)(2,1)S(1)}, bf16[2,4,128,576]{2,1,3,0:T(4,128)(2,1)}, u32[]{:S(2)}) copy-start(bf16[2,4,128,576]{2,1,3,0:T(4,128)(2,1)} %copy-done.1) | copy-start | bytes 3538948
  140.8 33.2 %all-to-all-start = ((f32[1,8,128,512]{3,1,0,2:T(8,128)}), f32[1,8,128,512]{3,1,0,2:T(8,128)}, u32[]{:S(2)}, u32[]{:S(2)}) async-start(f32[1,8,128,512]{3,1,0,2:T(8,128)} %copy.77), calls=%async_computation | async-start | bytes 4194304 | tf_op jit(solution)/shard_map/all_to_all | solution.py:99
  145.6 1.4 copy-start.9
  145.6 169.1 %all-reduce.5.cloned.1.call-start = ((), (), s32[]{:S(2)}) async-start(), calls=%async_computation.3 | async-start | bytes 458752 | tf_op jit(solution)/shard_map/psum | solution.py:144
  147.0 2.3 copy-start.10
  149.3 50.6 %copy-start.6 = (bf16[4,512,128]{2,1,0:T(8,128)(2,1)S(1)}, bf16[4,512,128]{2,1,0:T(8,128)(2,1)}, u32[]{:S(2)}) copy-start(bf16[4,512,128]{2,1,0:T(8,128)(2,1)} %param.23) | copy-start | bytes 1572868
  174.0 140.7 %copy-start.7 = (bf16[64,896]{1,0:T(8,128)(2,1)S(1)}, bf16[64,896]{1,0:T(8,128)(2,1)}, u32[]{:S(2)}) copy-start(bf16[64,896]{1,0:T(8,128)(2,1)} %param.25) | copy-start | bytes 344068
  177.1 138.7 %copy-start.5 = (bf16[896,576]{0,1:T(8,128)(2,1)S(1)}, bf16[896,576]{0,1:T(8,128)(2,1)}, u32[]{:S(2)}) copy-start(bf16[896,576]{0,1:T(8,128)(2,1)} %param.28) | copy-start | bytes 3096580
  177.1 138.7 %copy-start.8 = (f32[896]{0:T(1024)S(1)}, f32[896]{0:T(1024)}, u32[]{:S(2)}) copy-start(f32[896]{0:T(1024)} %param.26) | copy-start | bytes 10756
  202.3 185.4 %all-reduce.9.cloned.1.call-start = ((), (), s32[]{:S(2)}) async-start(), calls=%async_computation.5 | async-start | bytes 655360 | tf_op jit(solution)/shard_map/psum | solution.py:151
  319.3 185.4 %all-reduce.7.cloned.1.call-start = ((), (), s32[]{:S(2)}) async-start(), calls=%async_computation.4 | async-start | bytes 458752 | tf_op jit(solution)/shard_map/psum | solution.py:155
Sparse Core Ops, SparseCore 0:
  202.4 112.2 all-reduce.4
  319.4 68.3 all-reduce.8
  391.0 113.6 all-reduce.6
where the time goes:
time: 515 us; the launch traced here: 513 us
  waiting for transfers between devices  316 us (61%)
  matrix products  76.6 us (15%)
  local copies, waits for them, and re-layouts  38.6 us (7%)
  blocking collectives  36.2 us (7%)
  starting transfers between devices  17.5 us (3%)
  between operations  14.5 us (3%)
  other arithmetic  13 us (3%)
    psum x1, waiting for transfers between devices, on_device(): down_sum = lax.psum(down_part, 'kv')  115 us
    psum x1, waiting for transfers between devices, on_device(): attended = lax.psum(attn_part, 'kv')  112 us
    psum x1, waiting for transfers between devices, on_device(): lax.psum((gate_part, up_part, square_part), 'dp')  54.6 us
    dot_general x16, matrix products, visit(): jnp.dot(weights.astype(jnp.bfloat16), key_block[:, :LAT], preferred_eleme...  36.5 us
    dot_general x16, matrix products, visit(): jnp.einsum('rc,kc->rk', query_rows, key_block, preferred_element_type=jnp...  30.6 us
    all_to_all x1, waiting for transfers between devices, on_device(): lax.all_to_all(local_acc[None], 'kv', split_axis=2, concat_axis=0, tiled=...  23.6 us
    all_gather x1, blocking collectives, on_device(): all_latents = lax.all_gather(latent_rows, 'dp', axis=0, tiled=True)  22.4 us
    unnamed x27, local copies, waits for them, and re-layouts  19.9 us
  transfers between devices with their start and end apart: 6, of which 6 were waited for; matrix products, arithmetic and copies ran while one was open for 2% of the time, Pallas kernels for 0%

commit v1 on v0

v1 whole, which is shorter than its diff:
```python
import functools

import jax
import jax.numpy as jnp
from jax import lax
from jax.experimental import pallas as pl
from jax.experimental.pallas import tpu as pltpu
from jax.sharding import PartitionSpec as P

D, LAT, ROPE, HD = 7168, 512, 64, 128
SEQ_DP, STEPS = 2, 4
W = LAT + ROPE
FF_DEV = 576
DC = 896
BF, F32 = jnp.bfloat16, jnp.float32
C2 = (HD + ROPE) ** (-0.5) * 1.4426950408889634
NEG = -1e30
FLOOR = -20000.0
N_KV, N_DP = 32, 8
N_TILE = 28
KC = 1024
CTX = 4096
NCH = CTX // KC
RB = 32
ROWS = 512
MW = 640
NT = (((1,), (1,)), ((), ()))


def kernel(
    len_ref, seq_ref, pos_ref, qt_hbm, dr_hbm, ct_hbm, wuv_hbm, wout_hbm, hid_hbm, gain_ref, wg_hbm, wu_hbm, wd_hbm,
    out_ref,
    qv, qs0, qs1, kv0, kv1, sc0, sc1, pb0, pb1, mrun, m2, lrun, acc0, acc1,
    drv, wuv, wout, hid, wg, wu, wd,
    send_a, recv_a, send_b, recv_b, send_c, recv_c, send_d, recv_d, send_e, recv_e, send_f, recv_f,
    send_g, recv_g, send_h, recv_h, resid_s,
    ksem, lsem, ssem, rsem,
):
    me = lax.axis_index("kv")
    my_dp = lax.axis_index("dp")
    qss, kvs, scs, pbs, accs = (qs0, qs1), (kv0, kv1), (sc0, sc1), (pb0, pb1), (acc0, acc1)

    def kcopy(s, j):
        return pltpu.make_async_copy(
            ct_hbm.at[s, :, pl.ds(j * KC, KC)], kvs[s].at[:, pl.ds(j * KC, KC)], ksem.at[s, j]
        )

    loads = [
        pltpu.make_async_copy(src, dst, lsem.at[i])
        for i, (src, dst) in enumerate(
            [(qt_hbm, qv), (dr_hbm, drv), (wuv_hbm, wuv), (wout_hbm, wout), (hid_hbm, hid), (wg_hbm, wg), (wu_hbm, wu), (wd_hbm, wd)]
        )
    ]
    loads[0].start()
    for s in range(2):
        for j in range(NCH):
            kcopy(s, j).start()
    for c in loads[1:]:
        c.start()

    barrier = pltpu.get_barrier_semaphore()

    def hello_kv(i, c):
        pl.semaphore_signal(barrier, inc=1, device_id=(lax.rem(me + i, N_KV), my_dp), device_id_type=pl.DeviceIdType.MESH)
        return c

    def hello_dp(i, c):
        pl.semaphore_signal(barrier, inc=1, device_id=(me, lax.rem(my_dp + i, N_DP)), device_id_type=pl.DeviceIdType.MESH)
        return c

    lax.fori_loop(1, N_KV, hello_kv, 0)
    lax.fori_loop(1, N_DP, hello_dp, 0)

    seqs = [seq_ref[t] for t in range(8)]
    ranks = []
    for t in range(8):
        rank = jnp.int32(0)
        for u in range(t):
            rank = rank + (seqs[u] == seqs[t]).astype(jnp.int32)
        ranks.append(rank)
    place = [seqs[t] * STEPS + ranks[t] for t in range(8)]
    idx = []
    for g in range(8):
        at = jnp.int32(0)
        for t in range(8):
            at = at + t * (place[t] == g).astype(jnp.int32)
        idx.append(at)

    pi = lax.broadcasted_iota(jnp.int32, (ROWS, ROWS), 0)
    pj = lax.broadcasted_iota(jnp.int32, (ROWS, ROWS), 1)
    blk = pi >> 4
    want = ((pi >> 2) & 3) * 128 + (((blk & 15) * 2 + (blk >> 4)) * 4) + (pi & 3)
    perm = jnp.where(pj == want, 1.0, 0.0).astype(BF)
    loads[0].wait()

    def sort_q(s):
        qt = jnp.concatenate([qv[idx[s * STEPS + r]] for r in range(STEPS)], axis=1)
        qss[s][...] = lax.dot_general(perm, qt, NT, preferred_element_type=F32).astype(BF)

    starts = [len_ref[s] - me * CTX for s in range(2)]

    def qk(s, j):
        kcopy(s, j).wait()
        r = jnp.dot(qss[s][...], kvs[s][:, j * KC:(j + 1) * KC], preferred_element_type=F32)
        pos = lax.broadcasted_iota(jnp.int32, (1, KC), 1) + j * KC
        r = jnp.where(pos < starts[s], r, NEG)
        scs[s][:, j * KC:(j + 1) * KC] = r
        mx = r[:, :128]
        for c in range(1, KC // 128):
            mx = jnp.maximum(mx, r[:, c * 128:(c + 1) * 128])
        mrun[s] = mx if j == 0 else jnp.maximum(mrun[s], mx)

    def fin(s):
        m = jnp.max(mrun[s], axis=1, keepdims=True) * C2
        m = jnp.maximum(m, FLOOR).astype(BF).astype(F32)
        m2[s] = jnp.broadcast_to(m, (ROWS, 128))

    def pv(s, j, lo, hi):
        for rb in range(lo // RB, hi // RB):
            rows = slice(rb * RB, (rb + 1) * RB)
            mm = m2[s, rows, :]
            l = jnp.zeros((RB, 128), F32) if j == 0 else lrun[s, rows, :]
            for c in range(KC // 128):
                p = jnp.exp2(scs[s][rows, j * KC + c * 128:j * KC + (c + 1) * 128] * C2 - mm)
                l = l + p
                pbs[j % 2][rows, c * 128:(c + 1) * 128] = p.astype(BF)
            lrun[s, rows, :] = l
        r = lax.dot_general(
            pbs[j % 2][lo:hi, :], kvs[s][:LAT, j * KC:(j + 1) * KC], NT, preferred_element_type=F32
        )
        if j == 0:
            accs[s][lo:hi, :] = r
        else:
            accs[s][lo:hi, :] += r

    def ship(s, c):
        rows = slice(c * 256, (c + 1) * 256)
        l = jnp.sum(lrun[s, rows, :], axis=1, keepdims=True)
        l_hi = l.astype(BF).astype(F32)
        lane = lax.broadcasted_iota(jnp.int32, (256, 128), 1)
        ext = jnp.where(lane < 32, m2[s, rows, :], jnp.where(lane < 64, l_hi, l - l_hi))
        send_a[s, c * 16:(c + 1) * 16, :, 0:LAT] = accs[s][rows, :].astype(BF).reshape(16, 16, LAT)
        send_a[s, c * 16:(c + 1) * 16, :, LAT:MW] = ext.astype(BF).reshape(16, 16, 128)

        def one(i, carry):
            chip = lax.rem(lax.div(me, 2) + i, 16)
            to = chip * 2 + c

            @pl.when(to != me)
            def _():
                pltpu.make_async_remote_copy(
                    send_a.at[s, c * 16 + chip], recv_a.at[s, me], ssem.at[0], rsem.at[s],
                    device_id=(to, my_dp), device_id_type=pl.DeviceIdType.MESH,
                ).start()

            @pl.when(to == me)
            def _():
                recv_a[s, me] = send_a[s, c * 16 + chip]

            return carry

        lax.fori_loop(0, 16, one, 0)

    sort_q(0)
    for j in range(NCH):
        qk(0, j)
    fin(0)
    sort_q(1)
    for j in range(NCH):
        qk(1, j)
        pv(0, j, 0, ROWS)
    pl.semaphore_wait(barrier, N_KV - 1 + N_DP - 1)
    ship(0, 0)
    ship(0, 1)
    fin(1)
    for c in range(2):
        for j in range(NCH):
            pv(1, j, c * 256, (c + 1) * 256)
        ship(1, c)

    loads[1].wait()
    drafts = drv[...].astype(F32)
    poss = [pos_ref[t] for t in range(8)]
    posg = [pos_ref[idx[g]] for g in range(8)]
    my_blk = lax.rem(me, 2) * 16 + lax.div(me, 2)
    d_score, d_max = [], []
    rowi = lax.broadcasted_iota(jnp.int32, (16, 1), 0) >> 2
    for s in range(2):
        q_own = qss[s][pl.ds(pl.multiple_of(my_blk * 16, 16), 16), :].astype(F32)
        my_pos = jnp.zeros((16, 1), jnp.int32)
        for r in range(STEPS):
            my_pos = jnp.where(rowi == r, posg[s * STEPS + r], my_pos)
        cols = []
        for t in range(8):
            sct = jnp.sum(q_own * drafts[t:t + 1, :], axis=1, keepdims=True) * C2
            limit = jnp.where(seqs[t] == s, poss[t], jnp.int32(2 ** 30))
            cols.append(jnp.where(my_pos >= limit, sct, NEG))
        d_score.append(cols)
        d_max.append(functools.reduce(jnp.maximum, cols))

    def landed(buf, sem, n):
        view = buf.at[pl.ds(0, n)]
        pltpu.make_async_copy(view, view, sem).wait()

    lats = []
    for s in range(2):
        landed(recv_a.at[s], rsem.at[s], N_KV - 1)
        ext = recv_a[s, :, :, LAT:MW].astype(F32)
        m_k = ext[:, :, 0:1]
        l_k = ext[:, :, 32:33] + ext[:, :, 64:65]
        top = jnp.maximum(jnp.max(m_k, axis=0), d_max[s])
        w_k = jnp.exp2(m_k - top[None])
        den = jnp.sum(w_k * l_k, axis=0)
        num = jnp.zeros((16, LAT), F32)
        for k in range(N_KV):
            num = num + w_k[k] * recv_a[s, k, :, 0:LAT].astype(F32)
        for t in range(8):
            p = jnp.exp2(d_score[s][t] - top)
            den = den + p
            num = num + p.astype(BF).astype(F32) * drafts[t:t + 1, :LAT]
        lats.append((num / den).astype(BF))
    lat = jnp.concatenate(lats, axis=0)

    loads[2].wait()
    hrow = lax.broadcasted_iota(jnp.int32, (32, 1), 0) & 3
    vals = jnp.concatenate(
        [jnp.where(hrow == h, jnp.dot(lat, wuv[h], preferred_element_type=F32), 0.0) for h in range(4)], axis=1
    ).astype(BF)
    ut = lax.broadcasted_iota(jnp.int32, (8, 32), 0)
    uc = lax.broadcasted_iota(jnp.int32, (8, 32), 1) >> 2
    want_at = jnp.zeros((8, 32), jnp.int32)
    for t in range(8):
        want_at = jnp.where(ut == t, place[t], want_at)
    unsort = jnp.where(uc == want_at, 1.0, 0.0).astype(BF)
    v8 = jnp.dot(unsort, vals, preferred_element_type=F32)
    send_b[...] = jnp.concatenate([v8[:, :256], v8[:, 256:]], axis=0).astype(BF)
    recv_b[my_dp] = send_b[...]

    def over_dp(src, dst, s_sem, r_sem):
        def one(i, c):
            to = lax.rem(my_dp + i, N_DP)
            pltpu.make_async_remote_copy(
                src(to), dst.at[my_dp], s_sem, r_sem, device_id=(me, to), device_id_type=pl.DeviceIdType.MESH
            ).start()
            return c

        lax.fori_loop(1, N_DP, one, 0)

    def scatter_kv(src, dst, s_sem, r_sem):
        def one(i, c):
            to = lax.rem(me + i, N_KV)

            @pl.when(to < N_TILE)
            def _():
                pltpu.make_async_remote_copy(
                    src.at[to], dst.at[me], s_sem, r_sem, device_id=(to, my_dp), device_id_type=pl.DeviceIdType.MESH
                ).start()

            return c

        lax.fori_loop(1, N_KV, one, 0)

    def gather_kv(src, dst, s_sem, r_sem):
        def one(i, c):
            to = lax.rem(me + i, N_KV)
            pltpu.make_async_remote_copy(
                src, dst.at[me], s_sem, r_sem, device_id=(to, my_dp), device_id_type=pl.DeviceIdType.MESH
            ).start()
            return c

        lax.fori_loop(1, N_KV, one, 0)

    def tiles(x, buf):
        xb = x.astype(BF)
        for rc in range(4):
            for ct in range(7):
                buf[rc * 7 + ct] = xb[rc * 16:(rc + 1) * 16, ct * 128:(ct + 1) * 128]

    def whole(buf):
        return jnp.concatenate(
            [jnp.concatenate([buf[rc * 7 + ct].astype(F32) for ct in range(7)], axis=1) for rc in range(4)], axis=0
        )

    over_dp(lambda to: send_b, recv_b, ssem.at[1], rsem.at[2])
    landed(recv_b, rsem.at[2], N_DP - 1)
    loads[3].wait()
    all_vals = []
    for d in range(N_DP):
        both = recv_b[d].astype(F32)
        all_vals.append(jnp.concatenate([both[:8], both[8:]], axis=1))
    all_vals = jnp.concatenate(all_vals, axis=0).astype(BF)
    tiles(jnp.dot(all_vals, wout[...], preferred_element_type=F32), send_c)
    scatter_kv(send_c, recv_c, ssem.at[2], rsem.at[3])
    loads[4].wait()

    @pl.when(me < N_TILE)
    def _():
        recv_c[me] = send_c[me]
        landed(recv_c, rsem.at[3], N_KV - 1)
        total = jnp.sum(recv_c[...].astype(F32), axis=0)
        rc, ct = lax.div(me, 7), lax.rem(me, 7)
        own = hid[pl.ds(pl.multiple_of(rc * 16, 16), 16), pl.ds(pl.multiple_of(ct * 128, 128), 128)]
        send_d[...] = (own.astype(F32) + total).astype(BF)
        recv_d[me] = send_d[...]
        gather_kv(send_d, recv_d, ssem.at[3], rsem.at[4])
        landed(recv_d, rsem.at[4], N_TILE - 1)

    @pl.when(me >= N_TILE)
    def _():
        landed(recv_d, rsem.at[4], N_TILE)

    resid = whole(recv_d)
    square = jnp.sum(resid * resid, axis=1, keepdims=True)
    sq_hi = square.astype(BF).astype(F32)
    scaled = (resid * gain_ref[...]).astype(BF)
    loads[5].wait()
    loads[6].wait()
    gate = lax.dot_general(scaled, wg[...], NT, preferred_element_type=F32)
    up = lax.dot_general(scaled, wu[...], NT, preferred_element_type=F32)
    gate = jnp.concatenate([gate, jnp.broadcast_to(sq_hi, (64, MW - FF_DEV))], axis=1)
    up = jnp.concatenate([up, jnp.broadcast_to(square - sq_hi, (64, MW - FF_DEV))], axis=1)
    for d in range(N_DP):
        rows = slice(d * 8, (d + 1) * 8)
        send_e[d] = jnp.concatenate([gate[rows], up[rows]], axis=0).astype(BF)
    over_dp(lambda to: send_e.at[to], recv_e, ssem.at[4], rsem.at[5])
    recv_e[my_dp] = send_e[my_dp]
    landed(recv_e, rsem.at[5], N_DP - 1)
    total = jnp.sum(recv_e[...].astype(F32), axis=0)
    sq = total[0:8, FF_DEV:FF_DEV + 1] + total[8:16, FF_DEV:FF_DEV + 1]
    inv = lax.rsqrt(sq / D + 1e-06)
    g = total[0:8, :FF_DEV] * inv
    u = total[8:16, :FF_DEV] * inv
    act = g / (1.0 + jnp.exp(-g)) * u
    right = jnp.concatenate([act[:, 384:], jnp.zeros((8, 192), F32)], axis=1)
    send_f[...] = jnp.concatenate([act[:, :384], right], axis=0).astype(BF)
    recv_f[my_dp] = send_f[...]
    over_dp(lambda to: send_f, recv_f, ssem.at[5], rsem.at[6])
    landed(recv_f, rsem.at[6], N_DP - 1)
    acts = []
    for d in range(N_DP):
        both = recv_f[d].astype(F32)
        acts.append(jnp.concatenate([both[:8], both[8:, :192]], axis=1))
    acts = jnp.concatenate(acts, axis=0).astype(BF)
    loads[7].wait()
    tiles(jnp.dot(acts, wd[...], preferred_element_type=F32), send_g)
    scatter_kv(send_g, recv_g, ssem.at[6], rsem.at[7])

    @pl.when(me < N_TILE)
    def _():
        recv_g[me] = send_g[me]
        landed(recv_g, rsem.at[7], N_KV - 1)
        total = jnp.sum(recv_g[...].astype(F32), axis=0)
        send_h[...] = (send_d[...].astype(F32) + total).astype(BF)
        recv_h[me] = send_h[...]
        gather_kv(send_h, recv_h, ssem.at[7], rsem.at[8])
        landed(recv_h, rsem.at[8], N_TILE - 1)

    @pl.when(me >= N_TILE)
    def _():
        landed(recv_h, rsem.at[8], N_TILE)

    for rc in range(4):
        for ct in range(7):
            out_ref[rc * 16:(rc + 1) * 16, ct * 128:(ct + 1) * 128] = recv_h[rc * 7 + ct]

    for s in range(2):
        landed(send_a.at[s], ssem.at[0], N_KV - 1)
    landed(recv_b, ssem.at[1], N_DP - 1)
    landed(recv_e, ssem.at[4], N_DP - 1)
    landed(recv_f, ssem.at[5], N_DP - 1)

    @pl.when(me < N_TILE)
    def _():
        landed(send_c, ssem.at[2], N_TILE - 1)
        landed(send_g, ssem.at[6], N_TILE - 1)
        landed(recv_c, ssem.at[3], N_KV - 1)
        landed(recv_g, ssem.at[7], N_KV - 1)

    @pl.when(me >= N_TILE)
    def _():
        landed(send_c, ssem.at[2], N_TILE)
        landed(send_g, ssem.at[6], N_TILE)


def on_device(queries, drafts, cache, lengths, row_seq, row_pos, w_uv, w_out, hidden, gain, w_gate, w_up, w_down):
    smem = pl.BlockSpec(memory_space=pltpu.SMEM)
    vmem = pl.BlockSpec(memory_space=pltpu.VMEM)
    hbm = pl.BlockSpec(memory_space=pl.ANY)
    v = pltpu.VMEM
    scratch = [
        v((8, W, 128), BF), v((ROWS, W), BF), v((ROWS, W), BF), v((W, CTX), BF), v((W, CTX), BF),
        v((ROWS, CTX), F32), v((ROWS, CTX), F32), v((ROWS, KC), BF), v((ROWS, KC), BF),
        v((2, ROWS, 128), F32), v((2, ROWS, 128), F32), v((2, ROWS, 128), F32), v((ROWS, LAT), F32), v((ROWS, LAT), F32),
        v((8, W), BF), v((4, LAT, HD), BF), v((4 * HD, DC), BF), v((64, DC), BF), v((FF_DEV, DC), BF), v((FF_DEV, DC), BF), v((FF_DEV, DC), BF),
        v((2, 32, 16, MW), BF), v((2, 32, 16, MW), BF),
        v((16, 256), BF), v((N_DP, 16, 256), BF),
        v((N_TILE, 16, 128), BF), v((N_KV, 16, 128), BF),
        v((16, 128), BF), v((N_TILE, 16, 128), BF),
        v((N_DP, 16, MW), BF), v((N_DP, 16, MW), BF),
        v((16, 384), BF), v((N_DP, 16, 384), BF),
        v((N_TILE, 16, 128), BF), v((N_KV, 16, 128), BF),
        v((16, 128), BF), v((N_TILE, 16, 128), BF), v((8, 128), F32),
        pltpu.SemaphoreType.DMA((2, NCH)), pltpu.SemaphoreType.DMA((8,)), pltpu.SemaphoreType.DMA((8,)), pltpu.SemaphoreType.DMA((9,)),
    ]
    return pl.pallas_call(
        kernel,
        out_shape=jax.ShapeDtypeStruct((64, DC), BF),
        in_specs=[smem] * 3 + [hbm] * 6 + [vmem] + [hbm] * 3,
        out_specs=vmem,
        scratch_shapes=scratch,
        compiler_params=pltpu.CompilerParams(
            collective_id=0, has_side_effects=True, vmem_limit_bytes=58 << 20
        ),
        name="verify_layer",
    )(
        lengths, row_seq, row_pos, jnp.swapaxes(queries, 1, 2), drafts, jnp.swapaxes(cache, 1, 2), w_uv, w_out, hidden,
        gain.reshape(1, DC), w_gate.T, w_up.T, w_down,
    )


def solution(mesh):
    placed = (
        P("dp", None, None),
        P("dp", None),
        P("dp", "kv", None),
        P("dp"),
        P("dp"),
        P("dp"),
        P("kv", None, None),
        P("kv", "dp"),
        P(None, "dp"),
        P("dp"),
        P("dp", "kv"),
        P("dp", "kv"),
        P("kv", "dp"),
    )
    return jax.shard_map(
        on_device, mesh=mesh, in_specs=placed, out_specs=P(None, "dp"), check_vma=False
    )
```

time: 515 us -> 81.6 us (0.16)
  waiting for transfers between devices: 316 us -> 0 us
  Pallas kernels: 0 us -> 78.7 us
  matrix products: 76.6 us -> 0 us
  blocking collectives: 36.2 us -> 0 us
  local copies, waits for them, and re-layouts: 38.6 us -> 2.82 us
  starting transfers between devices: 17.5 us -> 0 us
  between operations: 14.5 us -> 0.01 us
  other arithmetic: 13 us -> 0 us
    psum x3 -> x0, waiting for transfers between devices: 282 us -> none  [the longest x1 115 us: on_device(): down_sum = lax.psum(down_part, 'kv')]
    pallas_call x0 -> x1, Pallas kernels: none -> 78.7 us  [on_device(): pl.pallas_call(kernel, out_shape=jax.ShapeDtypeStruct((64, DC), BF), in_s...]
    dot_general x42 -> x0, matrix products: 76.6 us -> none  [the longest x16 36.5 us: visit(): jnp.dot(weights.astype(jnp.bfloat16), key_block[:, :LAT], preferred_eleme...]
    all_to_all x3 -> x0, waiting for transfers between devices: 33.7 us -> none  [the longest x1 23.6 us: on_device(): lax.all_to_all(local_acc[None], 'kv', split_axis=2, concat_axis=0, tiled=...]
    all_gather x1 -> x0, blocking collectives: 22.4 us -> none  [on_device(): all_latents = lax.all_gather(latent_rows, 'dp', axis=0, tiled=True)]
    unnamed x27 -> x1, local copies, waits for them, and re-layouts: 19.9 us -> 1.55 us
    all_to_all x3 -> x0, starting transfers between devices: 17.2 us -> none  [the longest x1 8.61 us: on_device(): lax.all_to_all(local_sum[None], 'kv', split_axis=2, concat_axis=0, tiled=...]
    psum x1 -> x0, blocking collectives: 13.8 us -> none  [on_device(): lax.psum((gate_part, up_part, square_part), 'dp')]
  transfers between devices with their start and end apart: 6 -> 0, of which waited for: 6 -> 0; matrix products, arithmetic and copies ran while one was open for 2% -> 0% of each run, Pallas kernels for 0% -> 0%
where the time goes in v1:
time: 81.6 us; the launch traced here: 81.5 us
  Pallas kernels  78.7 us (96%)
  local copies, waits for them, and re-layouts  2.82 us (3%)
    pallas_call x1, Pallas kernels, on_device(): pl.pallas_call(kernel, out_shape=jax.ShapeDtypeStruct((64, DC), BF), in_s...  78.7 us

profile of v1, /device:TPU:1, one launch (start us, length us, event | category | flops | bytes accessed | tf_op | source)
XLA Modules:
  0.0 81.5 jit_solution(870573614620054635)
XLA Ops:
  0.0 1.3 %reshape.3.gain_ref = f32[1,896]{1,0:T(1,128)} reshape(f32[896]{0:T(1024)} %param.22) | data formatting | bytes 7168 | tf_op jit(solution)/shard_map/reshape | solution.py:417
  1.3 78.7 %verify_layer.1 = bf16[64,896]{1,0:T(8,128)(2,1)} custom-call(s32[2]{0:T(128)} %len_ref.1, s32[8]{0:T(128)} %seq_ref.1, s32[8]{0:T(128)} %pos_ref.1, bf16[8,576,128]{2,1,0:T(8,128)(2,1)} %bitcast.5, bf16[8,576]{1,0:T(8,128)(2,1)} %dr_hbm.1, bf16[2,576,4096]{2,1,0:T(8,128)(2,1)} %bitcast.4, bf16[4,512,128]{2,1,0:T(8,128)(2,1)} %wuv_hbm.1, ...), custom_call_target="tpu_custom_call" | custom-call | tf_op jit(solution)/shard_map/verify_layer/pallas_call | solution.py:405
  79.9 1.6 %copy.15 = bf16[64,896]{1,0:T(8,128)(2,1)} copy(bf16[64,896]{1,0:T(8,128)(2,1)} %verify_layer.1) | data formatting | bytes 229376

commit v2 on v1

--- a/solution.py
+++ b/solution.py
@@ -25,6 +25,9 @@
 ROWS = 512
 MW = 640
 NT = (((1,), (1,)), ((), ()))
+Z_FAR = (4, 3, 5, 2, 6, 1, 7)
+XY_FAR = sorted(((dx, dy) for dx in range(4) for dy in range(4)), key=lambda o: -(min(o[0], 4 - o[0]) + min(o[1], 4 - o[1])))
+KV_FAR = [(dx, dy, dc) for dx, dy in XY_FAR for dc in (0, 1)][:-2] + [(0, 0, 1)]
 
 
 def kernel(
@@ -32,12 +35,17 @@
     out_ref,
     qv, qs0, qs1, kv0, kv1, sc0, sc1, pb0, pb1, mrun, m2, lrun, acc0, acc1,
     drv, wuv, wout, hid, wg, wu, wd,
-    send_a, recv_a, send_b, recv_b, send_c, recv_c, send_d, recv_d, send_e, recv_e, send_f, recv_f,
-    send_g, recv_g, send_h, recv_h, resid_s,
+    send_s, recv_s, send_a, recv_a, send_b, recv_b, send_c, recv_c, send_d, recv_d, send_e, recv_e, send_f, recv_f,
+    send_g, recv_g, send_h,
     ksem, lsem, ssem, rsem,
 ):
     me = lax.axis_index("kv")
     my_dp = lax.axis_index("dp")
+    my_core = lax.rem(me, 2)
+    my_chip = lax.div(me, 2)
+    xs = [lax.rem(lax.div(me, 8) + dx, 4) * 8 for dx in range(4)]
+    ys = [lax.rem(lax.rem(my_chip, 4) + dy, 4) * 2 for dy in range(4)]
+    cs = [lax.rem(me + dc, 2) for dc in range(2)]
     qss, kvs, scs, pbs, accs = (qs0, qs1), (kv0, kv1), (sc0, sc1), (pb0, pb1), (acc0, acc1)
 
     def kcopy(s, j):
@@ -60,16 +68,17 @@
 
     barrier = pltpu.get_barrier_semaphore()
 
-    def hello_kv(i, c):
-        pl.semaphore_signal(barrier, inc=1, device_id=(lax.rem(me + i, N_KV), my_dp), device_id_type=pl.DeviceIdType.MESH)
-        return c
-
-    def hello_dp(i, c):
-        pl.semaphore_signal(barrier, inc=1, device_id=(me, lax.rem(my_dp + i, N_DP)), device_id_type=pl.DeviceIdType.MESH)
-        return c
-
-    lax.fori_loop(1, N_KV, hello_kv, 0)
-    lax.fori_loop(1, N_DP, hello_dp, 0)
+    def hello():
+        for dx, dy, dc in KV_FAR:
+            pl.semaphore_signal(
+                barrier, inc=1, device_id=(xs[dx] + ys[dy] + cs[dc], my_dp), device_id_type=pl.DeviceIdType.MESH
+            )
+        for dz in Z_FAR:
+            pl.semaphore_signal(
+                barrier, inc=1, device_id=(me, lax.rem(my_dp + dz, N_DP)), device_id_type=pl.DeviceIdType.MESH
+            )
+
+    hello()
 
     seqs = [seq_ref[t] for t in range(8)]
     ranks = []
@@ -86,11 +95,14 @@
             at = at + t * (place[t] == g).astype(jnp.int32)
         idx.append(at)
 
-    pi = lax.broadcasted_iota(jnp.int32, (ROWS, ROWS), 0)
-    pj = lax.broadcasted_iota(jnp.int32, (ROWS, ROWS), 1)
-    blk = pi >> 4
-    want = ((pi >> 2) & 3) * 128 + (((blk & 15) * 2 + (blk >> 4)) * 4) + (pi & 3)
-    perm = jnp.where(pj == want, 1.0, 0.0).astype(BF)
+    pi = lax.broadcasted_iota(jnp.int32, (ROWS, 128), 0)
+    pj = lax.broadcasted_iota(jnp.int32, (ROWS, 128), 1)
+    blk = (pi >> 4) & 15
+    owner = jnp.where(pi < 256, cs[1], cs[0])
+    for b, (dx, dy) in enumerate(XY_FAR):
+        owner = owner + jnp.where(blk == b, xs[dx] + ys[dy], 0)
+    want = ((pi >> 2) & 3) * 128 + owner * 4 + (pi & 3)
+    perm = jnp.concatenate([jnp.where(pj + 128 * r == want, 1.0, 0.0).astype(BF) for r in range(STEPS)], axis=1)
     loads[0].wait()
 
     def sort_q(s):
@@ -133,33 +145,47 @@
         else:
             accs[s][lo:hi, :] += r
 
-    def ship(s, c):
-        rows = slice(c * 256, (c + 1) * 256)
-        l = jnp.sum(lrun[s, rows, :], axis=1, keepdims=True)
+    def landed(buf, sem, n):
+        view = buf.at[pl.ds(0, n)]
+        pltpu.make_async_copy(view, view, sem).wait()
+
+    def pack(buf, acc, m, l):
+        lane = lax.broadcasted_iota(jnp.int32, m.shape, 1)
         l_hi = l.astype(BF).astype(F32)
-        lane = lax.broadcasted_iota(jnp.int32, (256, 128), 1)
-        ext = jnp.where(lane < 32, m2[s, rows, :], jnp.where(lane < 64, l_hi, l - l_hi))
-        send_a[s, c * 16:(c + 1) * 16, :, 0:LAT] = accs[s][rows, :].astype(BF).reshape(16, 16, LAT)
-        send_a[s, c * 16:(c + 1) * 16, :, LAT:MW] = ext.astype(BF).reshape(16, 16, 128)
-
-        def one(i, carry):
-            chip = lax.rem(lax.div(me, 2) + i, 16)
-            to = chip * 2 + c
-
-            @pl.when(to != me)
-            def _():
-                pltpu.make_async_remote_copy(
-                    send_a.at[s, c * 16 + chip], recv_a.at[s, me], ssem.at[0], rsem.at[s],
-                    device_id=(to, my_dp), device_id_type=pl.DeviceIdType.MESH,
-                ).start()
-
-            @pl.when(to == me)
-            def _():
-                recv_a[s, me] = send_a[s, c * 16 + chip]
-
-            return carry
-
-        lax.fori_loop(0, 16, one, 0)
+        ext = jnp.where(lane < 32, m, jnp.where(lane < 64, l_hi, l - l_hi))
+        buf[:, :, 0:LAT] = acc.astype(BF).reshape(-1, 16, LAT)
+        buf[:, :, LAT:MW] = ext.astype(BF).reshape(-1, 16, 128)
+
+    def total(s, rows):
+        return jnp.sum(lrun[s, rows, :], axis=1, keepdims=True)
+
+    def to_sibling(s):
+        rows = slice(0, 256)
+        pack(send_s.at[s], accs[s][rows, :], m2[s, rows, :], total(s, rows))
+        pltpu.make_async_remote_copy(
+            send_s.at[s], recv_s.at[s], ssem.at[8], rsem.at[9 + s], device_id=(xs[0] + ys[0] + cs[1], my_dp),
+            device_id_type=pl.DeviceIdType.MESH,
+        ).start()
+
+    def to_owners(s, lo, hi):
+        rows = slice(256 + lo * 16, 256 + hi * 16)
+        m_a = m2[s, rows, :]
+        ext = recv_s[s, lo:hi, :, LAT:MW].astype(F32).reshape(-1, 128)
+        m_b = ext[:, 0:1]
+        l_b = ext[:, 32:33] + ext[:, 64:65]
+        top = jnp.maximum(m_a, m_b)
+        w_a = jnp.exp2(m_a - top)
+        w_b = jnp.exp2(m_b - top)
+        acc = accs[s][rows, :] * w_a[:, 0:1] + recv_s[s, lo:hi, :, 0:LAT].astype(F32).reshape(-1, LAT) * w_b[:, 0:1]
+        pack(send_a.at[s, lo:hi], acc, top, total(s, rows) * w_a + l_b * w_b)
+        for b in range(lo, min(hi, 15)):
+            dx, dy = XY_FAR[b]
+            pltpu.make_async_remote_copy(
+                send_a.at[s, b], recv_a.at[s, b], ssem.at[0], rsem.at[s], device_id=(xs[dx] + ys[dy] + cs[0], my_dp),
+                device_id_type=pl.DeviceIdType.MESH,
+            ).start()
+        if hi == 16:
+            recv_a[s, 15] = send_a[s, 15]
 
     sort_q(0)
     for j in range(NCH):
@@ -167,26 +193,35 @@
     fin(0)
     sort_q(1)
     for j in range(NCH):
-        qk(1, j)
+        if j % 2 == 0:
+            qk(1, j // 2)
         pv(0, j, 0, ROWS)
     pl.semaphore_wait(barrier, N_KV - 1 + N_DP - 1)
-    ship(0, 0)
-    ship(0, 1)
+    to_sibling(0)
+    qk(1, 2)
+    qk(1, 3)
+    landed(recv_s.at[0], rsem.at[9], 16)
+    to_owners(0, 0, 16)
     fin(1)
-    for c in range(2):
-        for j in range(NCH):
-            pv(1, j, c * 256, (c + 1) * 256)
-        ship(1, c)
+    for j in range(NCH):
+        pv(1, j, 0, 256)
+    to_sibling(1)
+    for j in range(NCH):
+        pv(1, j, 256, 384)
+    landed(recv_s.at[1], rsem.at[10], 16)
+    to_owners(1, 0, 8)
+    for j in range(NCH):
+        pv(1, j, 384, 512)
+    to_owners(1, 8, 16)
 
     loads[1].wait()
     drafts = drv[...].astype(F32)
     poss = [pos_ref[t] for t in range(8)]
     posg = [pos_ref[idx[g]] for g in range(8)]
-    my_blk = lax.rem(me, 2) * 16 + lax.div(me, 2)
     d_score, d_max = [], []
     rowi = lax.broadcasted_iota(jnp.int32, (16, 1), 0) >> 2
     for s in range(2):
-        q_own = qss[s][pl.ds(pl.multiple_of(my_blk * 16, 16), 16), :].astype(F32)
+        q_own = qss[s][496:512, :].astype(F32)
         my_pos = jnp.zeros((16, 1), jnp.int32)
         for r in range(STEPS):
             my_pos = jnp.where(rowi == r, posg[s * STEPS + r], my_pos)
@@ -198,13 +233,9 @@
         d_score.append(cols)
         d_max.append(functools.reduce(jnp.maximum, cols))
 
-    def landed(buf, sem, n):
-        view = buf.at[pl.ds(0, n)]
-        pltpu.make_async_copy(view, view, sem).wait()
-
     lats = []
     for s in range(2):
-        landed(recv_a.at[s], rsem.at[s], N_KV - 1)
+        landed(recv_a.at[s], rsem.at[s], 15)
         ext = recv_a[s, :, :, LAT:MW].astype(F32)
         m_k = ext[:, :, 0:1]
         l_k = ext[:, :, 32:33] + ext[:, :, 64:65]
@@ -212,7 +243,7 @@
         w_k = jnp.exp2(m_k - top[None])
         den = jnp.sum(w_k * l_k, axis=0)
         num = jnp.zeros((16, LAT), F32)
-        for k in range(N_KV):
+        for k in range(16):
             num = num + w_k[k] * recv_a[s, k, :, 0:LAT].astype(F32)
         for t in range(8):
             p = jnp.exp2(d_score[s][t] - top)
@@ -237,18 +268,15 @@
     recv_b[my_dp] = send_b[...]
 
     def over_dp(src, dst, s_sem, r_sem):
-        def one(i, c):
-            to = lax.rem(my_dp + i, N_DP)
+        for dz in Z_FAR:
+            to = lax.rem(my_dp + dz, N_DP)
             pltpu.make_async_remote_copy(
                 src(to), dst.at[my_dp], s_sem, r_sem, device_id=(me, to), device_id_type=pl.DeviceIdType.MESH
             ).start()
-            return c
-
-        lax.fori_loop(1, N_DP, one, 0)
 
     def scatter_kv(src, dst, s_sem, r_sem):
-        def one(i, c):
-            to = lax.rem(me + i, N_KV)
+        for dx, dy, dc in KV_FAR:
+            to = xs[dx] + ys[dy] + cs[dc]
 
             @pl.when(to < N_TILE)
             def _():
@@ -256,19 +284,12 @@
                     src.at[to], dst.at[me], s_sem, r_sem, device_id=(to, my_dp), device_id_type=pl.DeviceIdType.MESH
                 ).start()
 
-            return c
-
-        lax.fori_loop(1, N_KV, one, 0)
-
     def gather_kv(src, dst, s_sem, r_sem):
-        def one(i, c):
-            to = lax.rem(me + i, N_KV)
+        for dx, dy, dc in KV_FAR:
+            to = xs[dx] + ys[dy] + cs[dc]
             pltpu.make_async_remote_copy(
                 src, dst.at[me], s_sem, r_sem, device_id=(to, my_dp), device_id_type=pl.DeviceIdType.MESH
             ).start()
-            return c
-
-        lax.fori_loop(1, N_KV, one, 0)
 
     def tiles(x, buf):
         xb = x.astype(BF)
@@ -312,7 +333,7 @@
     resid = whole(recv_d)
     square = jnp.sum(resid * resid, axis=1, keepdims=True)
     sq_hi = square.astype(BF).astype(F32)
-    scaled = (resid * gain_ref[...]).astype(BF)
+    scaled = (resid * gain_ref[...][None, :]).astype(BF)
     loads[5].wait()
     loads[6].wait()
     gate = lax.dot_general(scaled, wg[...], NT, preferred_element_type=F32)
@@ -351,20 +372,20 @@
         landed(recv_g, rsem.at[7], N_KV - 1)
         total = jnp.sum(recv_g[...].astype(F32), axis=0)
         send_h[...] = (send_d[...].astype(F32) + total).astype(BF)
-        recv_h[me] = send_h[...]
-        gather_kv(send_h, recv_h, ssem.at[7], rsem.at[8])
-        landed(recv_h, rsem.at[8], N_TILE - 1)
+        gather_kv(send_h, out_ref, ssem.at[7], rsem.at[8])
+        mine = pltpu.make_async_copy(send_h, out_ref.at[me], lsem.at[8])
+        mine.start()
+        mine.wait()
+        landed(out_ref, rsem.at[8], N_TILE - 1)
 
     @pl.when(me >= N_TILE)
     def _():
-        landed(recv_h, rsem.at[8], N_TILE)
-
-    for rc in range(4):
-        for ct in range(7):
-            out_ref[rc * 16:(rc + 1) * 16, ct * 128:(ct + 1) * 128] = recv_h[rc * 7 + ct]
+        landed(out_ref, rsem.at[8], N_TILE)
+
 
     for s in range(2):
-        landed(send_a.at[s], ssem.at[0], N_KV - 1)
+        landed(send_a.at[s], ssem.at[0], 15)
+        landed(send_s.at[s], ssem.at[8], 16)
     landed(recv_b, ssem.at[1], N_DP - 1)
     landed(recv_e, ssem.at[4], N_DP - 1)
     landed(recv_f, ssem.at[5], N_DP - 1)
@@ -392,30 +413,31 @@
         v((ROWS, CTX), F32), v((ROWS, CTX), F32), v((ROWS, KC), BF), v((ROWS, KC), BF),
         v((2, ROWS, 128), F32), v((2, ROWS, 128), F32), v((2, ROWS, 128), F32), v((ROWS, LAT), F32), v((ROWS, LAT), F32),
         v((8, W), BF), v((4, LAT, HD), BF), v((4 * HD, DC), BF), v((64, DC), BF), v((FF_DEV, DC), BF), v((FF_DEV, DC), BF), v((FF_DEV, DC), BF),
-        v((2, 32, 16, MW), BF), v((2, 32, 16, MW), BF),
+        v((2, 16, 16, MW), BF), v((2, 16, 16, MW), BF), v((2, 16, 16, MW), BF), v((2, 16, 16, MW), BF),
         v((16, 256), BF), v((N_DP, 16, 256), BF),
         v((N_TILE, 16, 128), BF), v((N_KV, 16, 128), BF),
         v((16, 128), BF), v((N_TILE, 16, 128), BF),
         v((N_DP, 16, MW), BF), v((N_DP, 16, MW), BF),
         v((16, 384), BF), v((N_DP, 16, 384), BF),
         v((N_TILE, 16, 128), BF), v((N_KV, 16, 128), BF),
-        v((16, 128), BF), v((N_TILE, 16, 128), BF), v((8, 128), F32),
-        pltpu.SemaphoreType.DMA((2, NCH)), pltpu.SemaphoreType.DMA((8,)), pltpu.SemaphoreType.DMA((8,)), pltpu.SemaphoreType.DMA((9,)),
+        v((16, 128), BF),
+        pltpu.SemaphoreType.DMA((2, NCH)), pltpu.SemaphoreType.DMA((9,)), pltpu.SemaphoreType.DMA((9,)), pltpu.SemaphoreType.DMA((11,)),
     ]
-    return pl.pallas_call(
+    out = pl.pallas_call(
         kernel,
-        out_shape=jax.ShapeDtypeStruct((64, DC), BF),
+        out_shape=jax.ShapeDtypeStruct((N_TILE, 16, 128), BF),
         in_specs=[smem] * 3 + [hbm] * 6 + [vmem] + [hbm] * 3,
-        out_specs=vmem,
+        out_specs=hbm,
         scratch_shapes=scratch,
         compiler_params=pltpu.CompilerParams(
-            collective_id=0, has_side_effects=True, vmem_limit_bytes=58 << 20
+            collective_id=0, has_side_effects=True, vmem_limit_bytes=60 << 20
         ),
         name="verify_layer",
     )(
         lengths, row_seq, row_pos, jnp.swapaxes(queries, 1, 2), drafts, jnp.swapaxes(cache, 1, 2), w_uv, w_out, hidden,
-        gain.reshape(1, DC), w_gate.T, w_up.T, w_down,
+        gain, w_gate.T, w_up.T, w_down,
     )
+    return out.reshape(4, 7, 16, 128).swapaxes(1, 2).reshape(64, DC)
 
 
 def solution(mesh):

time: 81.6 us -> 70.9 us (0.87)
  Pallas kernels: 78.7 us -> 69.2 us
  local copies, waits for them, and re-layouts: 2.82 us -> 1.6 us
    pallas_call x1, Pallas kernels: 78.7 us -> 69.2 us  [on_device(): pl.pallas_call(kernel, out_shape=jax.ShapeDtypeStruct((N_TILE, 16, 128),...]
    unnamed x1, local copies, waits for them, and re-layouts: 1.55 us -> 0.66 us
where the time goes in v2:
time: 70.9 us; the launch traced here: 70.8 us
  Pallas kernels  69.2 us (98%)
  local copies, waits for them, and re-layouts  1.6 us (2%)
    pallas_call x1, Pallas kernels, on_device(): pl.pallas_call(kernel, out_shape=jax.ShapeDtypeStruct((N_TILE, 16, 128),...  69.2 us

profile of v2, /device:TPU:1, one launch (start us, length us, event | category | flops | bytes accessed | tf_op | source)
XLA Modules:
  0.0 70.8 jit_solution(2650423257689964569)
XLA Ops:
  0.0 69.2 %verify_layer.1 = bf16[28,16,128]{2,1,0:T(8,128)(2,1)} custom-call(s32[2]{0:T(128)} %len_ref.1, s32[8]{0:T(128)} %seq_ref.1, s32[8]{0:T(128)} %pos_ref.1, bf16[8,576,128]{2,1,0:T(8,128)(2,1)} %bitcast.12, bf16[8,576]{1,0:T(8,128)(2,1)} %dr_hbm.1, bf16[2,576,4096]{2,1,0:T(8,128)(2,1)} %bitcast.11, bf16[4,512,128]{2,1,0:T(8,128)(2,1)} %wuv_hbm.1, ...), custom_call_target="tpu_custom_call" | custom-call | tf_op jit(solution)/shard_map/verify_layer/pallas_call | solution.py:426
  69.2 0.9 %copy.15 = bf16[4,7,16,128]{3,1,2,0:T(8,128)(2,1)S(1)} copy(bf16[4,7,16,128]{3,2,1,0:T(8,128)(2,1)} %bitcast.16) | data formatting | bytes 229376 | tf_op jit(solution)/shard_map/reshape | solution.py:440
  70.2 0.7 copy.18

commit v3 on v2

--- a/solution.py
+++ b/solution.py
@@ -21,6 +21,8 @@
 KC = 1024
 CTX = 4096
 NCH = CTX // KC
+KP = 2048
+NPV = CTX // KP
 RB = 32
 ROWS = 512
 MW = 640
@@ -34,9 +36,9 @@
     len_ref, seq_ref, pos_ref, qt_hbm, dr_hbm, ct_hbm, wuv_hbm, wout_hbm, hid_hbm, gain_ref, wg_hbm, wu_hbm, wd_hbm,
     out_ref,
     qv, qs0, qs1, kv0, kv1, sc0, sc1, pb0, pb1, mrun, m2, lrun, acc0, acc1,
-    drv, wuv, wout, hid, wg, wu, wd,
-    send_s, recv_s, send_a, recv_a, send_b, recv_b, send_c, recv_c, send_d, recv_d, send_e, recv_e, send_f, recv_f,
-    send_g, recv_g, send_h,
+    drv, wuv, wout, hid, wg, wu, wd, wgt, wut,
+    send_s, recv_s, send_a, recv_a, send_b, recv_b, send_c, recv_c, send_d, recv_d, send_e, recv_e, send_x, recv_x, send_f, recv_f,
+    send_g, recv_g, send_h, count_h,
     ksem, lsem, ssem, rsem,
 ):
     me = lax.axis_index("kv")
@@ -115,7 +117,7 @@
         kcopy(s, j).wait()
         r = jnp.dot(qss[s][...], kvs[s][:, j * KC:(j + 1) * KC], preferred_element_type=F32)
         pos = lax.broadcasted_iota(jnp.int32, (1, KC), 1) + j * KC
-        r = jnp.where(pos < starts[s], r, NEG)
+        r = jnp.where(pos < starts[s], r * C2, NEG)
         scs[s][:, j * KC:(j + 1) * KC] = r
         mx = r[:, :128]
         for c in range(1, KC // 128):
@@ -123,7 +125,7 @@
         mrun[s] = mx if j == 0 else jnp.maximum(mrun[s], mx)
 
     def fin(s):
-        m = jnp.max(mrun[s], axis=1, keepdims=True) * C2
+        m = jnp.max(mrun[s], axis=1, keepdims=True)
         m = jnp.maximum(m, FLOOR).astype(BF).astype(F32)
         m2[s] = jnp.broadcast_to(m, (ROWS, 128))
 
@@ -132,13 +134,13 @@
             rows = slice(rb * RB, (rb + 1) * RB)
             mm = m2[s, rows, :]
             l = jnp.zeros((RB, 128), F32) if j == 0 else lrun[s, rows, :]
-            for c in range(KC // 128):
-                p = jnp.exp2(scs[s][rows, j * KC + c * 128:j * KC + (c + 1) * 128] * C2 - mm)
+            for c in range(KP // 128):
+                p = jnp.exp2(scs[s][rows, j * KP + c * 128:j * KP + (c + 1) * 128] - mm)
                 l = l + p
                 pbs[j % 2][rows, c * 128:(c + 1) * 128] = p.astype(BF)
             lrun[s, rows, :] = l
         r = lax.dot_general(
-            pbs[j % 2][lo:hi, :], kvs[s][:LAT, j * KC:(j + 1) * KC], NT, preferred_element_type=F32
+            pbs[j % 2][lo:hi, :], kvs[s][:LAT, j * KP:(j + 1) * KP], NT, preferred_element_type=F32
         )
         if j == 0:
             accs[s][lo:hi, :] = r
@@ -192,9 +194,8 @@
         qk(0, j)
     fin(0)
     sort_q(1)
-    for j in range(NCH):
-        if j % 2 == 0:
-            qk(1, j // 2)
+    for j in range(NPV):
+        qk(1, j)
         pv(0, j, 0, ROWS)
     pl.semaphore_wait(barrier, N_KV - 1 + N_DP - 1)
     to_sibling(0)
@@ -203,16 +204,21 @@
     landed(recv_s.at[0], rsem.at[9], 16)
     to_owners(0, 0, 16)
     fin(1)
-    for j in range(NCH):
+    for j in range(NPV):
         pv(1, j, 0, 256)
     to_sibling(1)
-    for j in range(NCH):
+    for j in range(NPV):
         pv(1, j, 256, 384)
     landed(recv_s.at[1], rsem.at[10], 16)
     to_owners(1, 0, 8)
-    for j in range(NCH):
+    for j in range(NPV):
         pv(1, j, 384, 512)
     to_owners(1, 8, 16)
+
+    loads[5].wait()
+    loads[6].wait()
+    wgt[...] = wg[...].T
+    wut[...] = wu[...].T
 
     loads[1].wait()
     drafts = drv[...].astype(F32)
@@ -288,7 +294,7 @@
         for dx, dy, dc in KV_FAR:
             to = xs[dx] + ys[dy] + cs[dc]
             pltpu.make_async_remote_copy(
-                src, dst.at[me], s_sem, r_sem, device_id=(to, my_dp), device_id_type=pl.DeviceIdType.MESH
+                src, dst, s_sem, r_sem, device_id=(to, my_dp), device_id_type=pl.DeviceIdType.MESH
             ).start()
 
     def tiles(x, buf):
@@ -323,7 +329,7 @@
         own = hid[pl.ds(pl.multiple_of(rc * 16, 16), 16), pl.ds(pl.multiple_of(ct * 128, 128), 128)]
         send_d[...] = (own.astype(F32) + total).astype(BF)
         recv_d[me] = send_d[...]
-        gather_kv(send_d, recv_d, ssem.at[3], rsem.at[4])
+        gather_kv(send_d, recv_d.at[me], ssem.at[3], rsem.at[4])
         landed(recv_d, rsem.at[4], N_TILE - 1)
 
     @pl.when(me >= N_TILE)
@@ -334,19 +340,27 @@
     square = jnp.sum(resid * resid, axis=1, keepdims=True)
     sq_hi = square.astype(BF).astype(F32)
     scaled = (resid * gain_ref[...][None, :]).astype(BF)
-    loads[5].wait()
-    loads[6].wait()
-    gate = lax.dot_general(scaled, wg[...], NT, preferred_element_type=F32)
-    up = lax.dot_general(scaled, wu[...], NT, preferred_element_type=F32)
+    gate = jnp.dot(scaled, wgt[:, :256], preferred_element_type=F32)
+    up = jnp.dot(scaled, wut[:, :256], preferred_element_type=F32)
+    for d in range(N_DP):
+        rows = slice(d * 8, (d + 1) * 8)
+        send_e[d] = jnp.concatenate([gate[rows], up[rows]], axis=0).astype(BF)
+    over_dp(lambda to: send_e.at[to], recv_e, ssem.at[4], rsem.at[5])
+    gate = jnp.dot(scaled, wgt[:, 256:], preferred_element_type=F32)
+    up = jnp.dot(scaled, wut[:, 256:], preferred_element_type=F32)
     gate = jnp.concatenate([gate, jnp.broadcast_to(sq_hi, (64, MW - FF_DEV))], axis=1)
     up = jnp.concatenate([up, jnp.broadcast_to(square - sq_hi, (64, MW - FF_DEV))], axis=1)
     for d in range(N_DP):
         rows = slice(d * 8, (d + 1) * 8)
-        send_e[d] = jnp.concatenate([gate[rows], up[rows]], axis=0).astype(BF)
-    over_dp(lambda to: send_e.at[to], recv_e, ssem.at[4], rsem.at[5])
+        send_x[d] = jnp.concatenate([gate[rows], up[rows]], axis=0).astype(BF)
+    over_dp(lambda to: send_x.at[to], recv_x, ssem.at[9], rsem.at[11])
     recv_e[my_dp] = send_e[my_dp]
+    recv_x[my_dp] = send_x[my_dp]
     landed(recv_e, rsem.at[5], N_DP - 1)
-    total = jnp.sum(recv_e[...].astype(F32), axis=0)
+    left = jnp.sum(recv_e[...].astype(F32), axis=0)
+    landed(recv_x, rsem.at[11], N_DP - 1)
+    right = jnp.sum(recv_x[...].astype(F32), axis=0)
+    total = jnp.concatenate([left, right], axis=1)
     sq = total[0:8, FF_DEV:FF_DEV + 1] + total[8:16, FF_DEV:FF_DEV + 1]
     inv = lax.rsqrt(sq / D + 1e-06)
     g = total[0:8, :FF_DEV] * inv
@@ -371,16 +385,18 @@
         recv_g[me] = send_g[me]
         landed(recv_g, rsem.at[7], N_KV - 1)
         total = jnp.sum(recv_g[...].astype(F32), axis=0)
-        send_h[...] = (send_d[...].astype(F32) + total).astype(BF)
-        gather_kv(send_h, out_ref, ssem.at[7], rsem.at[8])
-        mine = pltpu.make_async_copy(send_h, out_ref.at[me], lsem.at[8])
+        done = send_d[...].astype(F32) + total
+        send_h[...] = done.astype(BF)
+        spot = out_ref.at[lax.rem(me, 7), pl.ds(pl.multiple_of(lax.div(me, 7) * 16, 16), 16)]
+        gather_kv(send_h, spot, ssem.at[7], rsem.at[8])
+        mine = pltpu.make_async_copy(send_h, spot, lsem.at[8])
         mine.start()
         mine.wait()
-        landed(out_ref, rsem.at[8], N_TILE - 1)
+        landed(count_h, rsem.at[8], N_TILE - 1)
 
     @pl.when(me >= N_TILE)
     def _():
-        landed(out_ref, rsem.at[8], N_TILE)
+        landed(count_h, rsem.at[8], N_TILE)
 
 
     for s in range(2):
@@ -388,6 +404,7 @@
         landed(send_s.at[s], ssem.at[8], 16)
     landed(recv_b, ssem.at[1], N_DP - 1)
     landed(recv_e, ssem.at[4], N_DP - 1)
+    landed(recv_x, ssem.at[9], N_DP - 1)
     landed(recv_f, ssem.at[5], N_DP - 1)
 
     @pl.when(me < N_TILE)
@@ -395,7 +412,7 @@
         landed(send_c, ssem.at[2], N_TILE - 1)
         landed(send_g, ssem.at[6], N_TILE - 1)
         landed(recv_c, ssem.at[3], N_KV - 1)
-        landed(recv_g, ssem.at[7], N_KV - 1)
+        landed(count_h, ssem.at[7], N_KV - 1)
 
     @pl.when(me >= N_TILE)
     def _():
@@ -410,22 +427,22 @@
     v = pltpu.VMEM
     scratch = [
         v((8, W, 128), BF), v((ROWS, W), BF), v((ROWS, W), BF), v((W, CTX), BF), v((W, CTX), BF),
-        v((ROWS, CTX), F32), v((ROWS, CTX), F32), v((ROWS, KC), BF), v((ROWS, KC), BF),
+        v((ROWS, CTX), F32), v((ROWS, CTX), F32), v((ROWS, KP), BF), v((ROWS, KP), BF),
         v((2, ROWS, 128), F32), v((2, ROWS, 128), F32), v((2, ROWS, 128), F32), v((ROWS, LAT), F32), v((ROWS, LAT), F32),
-        v((8, W), BF), v((4, LAT, HD), BF), v((4 * HD, DC), BF), v((64, DC), BF), v((FF_DEV, DC), BF), v((FF_DEV, DC), BF), v((FF_DEV, DC), BF),
+        v((8, W), BF), v((4, LAT, HD), BF), v((4 * HD, DC), BF), v((64, DC), BF), v((FF_DEV, DC), BF), v((FF_DEV, DC), BF), v((FF_DEV, DC), BF), v((DC, FF_DEV), BF), v((DC, FF_DEV), BF),
         v((2, 16, 16, MW), BF), v((2, 16, 16, MW), BF), v((2, 16, 16, MW), BF), v((2, 16, 16, MW), BF),
         v((16, 256), BF), v((N_DP, 16, 256), BF),
         v((N_TILE, 16, 128), BF), v((N_KV, 16, 128), BF),
         v((16, 128), BF), v((N_TILE, 16, 128), BF),
-        v((N_DP, 16, MW), BF), v((N_DP, 16, MW), BF),
+        v((N_DP, 16, 256), BF), v((N_DP, 16, 256), BF), v((N_DP, 16, 384), BF), v((N_DP, 16, 384), BF),
         v((16, 384), BF), v((N_DP, 16, 384), BF),
         v((N_TILE, 16, 128), BF), v((N_KV, 16, 128), BF),
-        v((16, 128), BF),
-        pltpu.SemaphoreType.DMA((2, NCH)), pltpu.SemaphoreType.DMA((9,)), pltpu.SemaphoreType.DMA((9,)), pltpu.SemaphoreType.DMA((11,)),
+        v((16, 128), BF), v((N_KV, 16, 128), BF),
+        pltpu.SemaphoreType.DMA((2, NCH)), pltpu.SemaphoreType.DMA((9,)), pltpu.SemaphoreType.DMA((10,)), pltpu.SemaphoreType.DMA((12,)),
     ]
     out = pl.pallas_call(
         kernel,
-        out_shape=jax.ShapeDtypeStruct((N_TILE, 16, 128), BF),
+        out_shape=jax.ShapeDtypeStruct((7, 64, 128), BF),
         in_specs=[smem] * 3 + [hbm] * 6 + [vmem] + [hbm] * 3,
         out_specs=hbm,
         scratch_shapes=scratch,
@@ -437,7 +454,7 @@
         lengths, row_seq, row_pos, jnp.swapaxes(queries, 1, 2), drafts, jnp.swapaxes(cache, 1, 2), w_uv, w_out, hidden,
         gain, w_gate.T, w_up.T, w_down,
     )
-    return out.reshape(4, 7, 16, 128).swapaxes(1, 2).reshape(64, DC)
+    return out.swapaxes(0, 1).reshape(64, DC)
 
 
 def solution(mesh):

time: 70.9 us -> 70.2 us (level)
  no operation moved by 1% of the time
where the time goes in v3:
time: 70.2 us; the launch traced here: 70.1 us
  Pallas kernels  68.5 us (98%)
  local copies, waits for them, and re-layouts  1.56 us (2%)
    pallas_call x1, Pallas kernels, on_device(): pl.pallas_call(kernel, out_shape=jax.ShapeDtypeStruct((7, 64, 128), BF),...  68.5 us
    reshape x1, local copies, waits for them, and re-layouts, on_device(): return out.swapaxes(0, 1).reshape(64, DC)  1.56 us

profile of v3, /device:TPU:1, one launch (start us, length us, event | category | flops | bytes accessed | tf_op | source)
XLA Modules:
  0.0 70.1 jit_solution(11530140259569056529)
XLA Ops:
  0.0 68.5 %verify_layer.1 = bf16[7,64,128]{2,1,0:T(8,128)(2,1)} custom-call(s32[2]{0:T(128)} %len_ref.1, s32[8]{0:T(128)} %seq_ref.1, s32[8]{0:T(128)} %pos_ref.1, bf16[8,576,128]{2,1,0:T(8,128)(2,1)} %bitcast.11, bf16[8,576]{1,0:T(8,128)(2,1)} %dr_hbm.1, bf16[2,576,4096]{2,1,0:T(8,128)(2,1)} %bitcast.10, bf16[4,512,128]{2,1,0:T(8,128)(2,1)} %wuv_hbm.1, ...), custom_call_target="tpu_custom_call" | custom-call | tf_op jit(solution)/shard_map/verify_layer/pallas_call | solution.py:443
  68.5 1.6 %copy_bitcast_fusion = bf16[64,896]{1,0:T(8,128)(2,1)} fusion(bf16[7,64,128]{2,1,0:T(8,128)(2,1)} %verify_layer.1), kind=kLoop, calls=%fused_computation | loop fusion | bytes 229376 | tf_op jit(solution)/shard_map/reshape | solution.py:457
